TPU v7x, 512 devices: a whole 4x4x16 slice. The times are simulated.
512 devices in a mesh: chan: 128 (over z, x, core), blk: 4 (over y).
Axes of the slice: x: 4, y: 4, z: 16, core: 2. Of those that a mesh axis runs over, the one named last changes fastest.
Arguments:
- omega: float32 [128, 576, 576], P('chan', 'blk'), may hold values from -0.25 to 0.25
- hamiltonian: float32 [128, 576, 576], P('chan', 'blk'), may hold values from -6 to 6
- pair_occ: float32 [128, 576], P('chan'), may hold values from -1 to 1
- cross_occ: float32 [128, 576], P('chan'), may hold values from -1 to 1
- block_size: int32 [128], P('chan'), may hold values from 288 to 576
- jlabel: int32 [128], replicated, may hold values from 0 to 127
- family: int32 [128], replicated, may hold values from 0 to 3
- sixj: float32 [128, 128], replicated, may hold values from -1 to 1
- column_map: int32 [576], replicated, may hold values from 0 to 575, each once
Outputs:
- evolved: float32 [128, 576, 576], P('chan', 'blk')
Inputs may be any that keep to these rules, and one draw needn't show every extreme that they name: `column_map`: a permutation of 0 to 575.
All inputs are finite; a program needn't handle non-finite values.
Results may differ from a plain program's by a relative error of at most 0.0032.
Values may be sent and summed in bfloat16 or wider, within the bound.
A program may use at most 64 MiB of HBM per device.

v0:
```python
import jax
import jax.numpy as jnp
from jax import lax
from jax.sharding import PartitionSpec as P

exact_mode = lax.Precision.HIGHEST


def in_order(parts, dim):
    parts = jnp.moveaxis(parts, 0, dim)
    lengths = parts.shape
    return parts.reshape(*lengths[:dim], lengths[dim] * lengths[dim + 1], *lengths[dim + 2 :])


def copy_for_each(shard, axis):
    copies = jnp.broadcast_to(shard, (lax.axis_size(axis), *shard.shape))
    return lax.all_to_all(copies, axis, split_axis=0, concat_axis=0, tiled=True)


def gather_directly(shard, axis, dim):
    return in_order(copy_for_each(shard, axis), dim)


def mixing_matrix(jlabel, family, sixj):
    levels = sixj.shape[0]
    one_hot = (jlabel[:, None] == jnp.arange(levels, dtype=jnp.int32)[None, :]).astype(jnp.float32)
    picked = jnp.dot(one_hot, sixj, precision=exact_mode, preferred_element_type=jnp.float32)
    picked = jnp.dot(picked, one_hot.T, precision=exact_mode, preferred_element_type=jnp.float32)
    kindred = (family[:, None] == family[None, :]).astype(jnp.float32)
    return picked * kindred


def commutator(left_rows, left_full, right_rows, weights):
    scaled_left = (left_rows * weights[:, None, :]).astype(jnp.bfloat16)
    scaled_right = (right_rows * weights[:, None, :]).astype(jnp.bfloat16)
    initial = -jnp.einsum(
        "crk,ckq->crq", scaled_right, left_full, preferred_element_type=jnp.float32
    )
    return initial + jnp.einsum(
        "crk,ckq->crq",
        scaled_left,
        lax.all_gather(right_rows.astype(jnp.bfloat16), "blk", axis=1, tiled=True),
        preferred_element_type=jnp.float32,
    )


def through_mixing(stacked, apply_fn):
    chan_size = lax.axis_size("chan")
    members, channels_here, rows_here, block_width = stacked.shape
    shaped = stacked.reshape(
        members, channels_here, chan_size, rows_here * block_width // chan_size
    )
    returned = lax.all_to_all(
        apply_fn(lax.all_to_all(shaped, "chan", split_axis=2, concat_axis=1, tiled=True)),
        "chan",
        split_axis=1,
        concat_axis=2,
        tiled=True,
    )
    return returned.reshape(returned.shape[0], channels_here, rows_here, block_width)


def on_device(
    omega, hamiltonian, pair_occ, cross_occ, block_size, jlabel, family, sixj, column_map
):
    channels_here, rows_here, block_width = omega.shape
    mixing = mixing_matrix(jlabel, family, sixj)
    row_index = lax.axis_index("blk") * rows_here + jnp.arange(rows_here, dtype=jnp.int32)
    col_index = jnp.arange(block_width, dtype=jnp.int32)
    inside_block = (row_index[None, :, None] < block_size[:, None, None]) & (
        col_index[None, None, :] < block_size[:, None, None]
    )
    window_mask = inside_block.astype(jnp.float32)
    generator = omega * window_mask
    start_ham = hamiltonian * window_mask
    inverse_map = jnp.argsort(column_map)

    def forward_mix(received):
        return jnp.einsum(
            "kc,scil->skil",
            mixing,
            received,
            precision=exact_mode,
            preferred_element_type=jnp.float32,
        )

    def reverse_mix(received):
        return jnp.einsum(
            "ck,scil->skil",
            mixing,
            received,
            precision=exact_mode,
            preferred_element_type=jnp.float32,
        )

    crossed = through_mixing(
        jnp.stack([generator[:, :, column_map], start_ham[:, :, column_map]]), forward_mix
    )
    gen_cross = crossed[0]
    ham_cross = crossed[1]
    gen_full = lax.all_gather(generator.astype(jnp.bfloat16), "blk", axis=1, tiled=True)
    first_pp = commutator(generator, gen_full, start_ham, pair_occ)
    cross_full = gather_directly(gen_cross.astype(jnp.bfloat16), "blk", 1)
    first_cc = commutator(gen_cross, cross_full, ham_cross, cross_occ)

    def both_mix(received):
        restored = jnp.einsum(
            "ck,cil->kil",
            mixing,
            received[1],
            precision=exact_mode,
            preferred_element_type=jnp.float32,
        )
        combined = jnp.einsum(
            "kc,cil->kil",
            mixing,
            received[0] + restored,
            precision=exact_mode,
            preferred_element_type=jnp.float32,
        )
        return jnp.stack([restored, combined])

    outcome = through_mixing(jnp.stack([first_pp[:, :, column_map], first_cc]), both_mix)
    eta = first_pp + outcome[0][:, :, inverse_map]
    eta_cross = outcome[1]
    second_pp = commutator(generator, gen_full, eta, pair_occ)
    second_cc = commutator(gen_cross, cross_full, eta_cross, cross_occ)
    second_back = through_mixing(second_cc[None], reverse_mix)[0]
    second = second_pp + second_back[:, :, inverse_map]
    return (start_ham + eta + 0.5 * second) * window_mask


def solution(mesh):
    in_specs = (
        P("chan", "blk", None),
        P("chan", "blk", None),
        P("chan", None),
        P("chan", None),
        P("chan"),
        P(),
        P(),
        P(),
        P(),
    )
    out_specs = P("chan", "blk", None)
    return jax.shard_map(
        on_device, mesh=mesh, in_specs=in_specs, out_specs=out_specs, check_vma=False
    )
```

profile of v0, /device:TPU:33, one launch (start us, length us, event | category | flops | bytes accessed | tf_op | source)
XLA Modules:
  0.0 370.8 jit_solution(17199406350710039180)
XLA Ops:
  0.8 1.2 fusion.21
  2.2 2.2 gather_fusion.1
  5.2 2.2 gather_fusion.2
  8.1 1.5 copy.68
  9.6 19.4 %all-to-all-start = ((f32[2,1,128,648]{3,0,1,2:T(2,128)}), f32[2,1,128,648]{3,0,1,2:T(2,128)S(1)}, u32[]{:S(2)}, u32[]{:S(2)}) async-start(f32[2,1,128,648]{3,0,1,2:T(2,128)} %copy.68), calls=%async_computation | async-start | bytes 1572864 | tf_op jit(solution)/shard_map/all_to_all | solution.py:54
  29.6 44.0 %all-to-all-done = f32[2,1,128,648]{3,0,1,2:T(2,128)S(1)} async-done(((f32[2,1,128,648]{3,0,1,2:T(2,128)}), f32[2,1,128,648]{3,0,1,2:T(2,128)S(1)}, u32[]{:S(2)}, u32[]{:S(2)}) %all-to-all-start) | async-done | bytes 663584 | tf_op jit(solution)/shard_map/all_to_all | solution.py:54
  74.9 1.3 copy.70
  76.2 6.8 %all-to-all-start.1 = ((f32[2,128,1,648]{3,0,2,1:T(2,128)}), f32[2,128,1,648]{3,0,2,1:T(2,128)}, u32[]{:S(2)}, u32[]{:S(2)}) async-start(f32[2,128,1,648]{3,0,2,1:T(2,128)} %copy.70), calls=%async_computation.1 | async-start | bytes 1572864 | tf_op jit(solution)/shard_map/all_to_all | solution.py:53
  85.1 12.4 %all_gather.15 = bf16[1,576,576]{2,1,0:T(8,128)(2,1)S(1)} all-gather(bf16[1,144,576]{2,1,0:T(8,128)(2,1)S(1)} %get-tuple-element.17), channel_id=1, replica_groups=mesh['chan'=128,'blk'=4] {'blk'}, dimensions={1}, use_global_device_ids=true | all-gather | bytes 829440 | tf_op jit(solution)/shard_map/all_gather | solution.py:101
  97.5 12.1 %all_gather.16 = bf16[1,576,576]{2,1,0:T(8,128)(2,1)S(1)} all-gather(bf16[1,144,576]{2,1,0:T(8,128)(2,1)S(1)} %get-tuple-element.18), channel_id=1, replica_groups=mesh['chan'=128,'blk'=4] {'blk'}, dimensions={1}, use_global_device_ids=true | all-gather | bytes 829440 | tf_op jit(solution)/shard_map/all_gather | solution.py:42
  110.6 2.2 gather_fusion
  114.1 13.2 %all-to-all-done.1 = f32[2,128,1,648]{3,0,2,1:T(2,128)} async-done(((f32[2,128,1,648]{3,0,2,1:T(2,128)}), f32[2,128,1,648]{3,0,2,1:T(2,128)}, u32[]{:S(2)}, u32[]{:S(2)}) %all-to-all-start.1) | async-done | bytes 663584 | tf_op jit(solution)/shard_map/all_to_all | solution.py:53
  127.4 2.0 fusion.44
  131.3 1.4 convert_element_type.100
  135.2 4.3 %all-to-all-start.2 = ((bf16[4,1,144,576]{3,2,1,0:T(8,128)(2,1)}), bf16[4,1,144,576]{3,2,1,0:T(8,128)(2,1)S(1)}, u32[]{:S(2)}, u32[]{:S(2)}) async-start(bf16[4,1,144,576]{3,2,1,0:T(8,128)(2,1)} %broadcast_in_dim.7), calls=%async_computation.2 | async-start | bytes 1474560 | tf_op jit(solution)/shard_map/all_to_all | solution.py:17
  139.5 18.4 %all_gather.17 = bf16[1,576,576]{2,1,0:T(8,128)(2,1)S(1)} all-gather(bf16[1,144,576]{2,1,0:T(8,128)(2,1)S(1)} %copy-done.12), channel_id=1, replica_groups=mesh['chan'=128,'blk'=4] {'blk'}, dimensions={1}, use_global_device_ids=true | all-gather | bytes 829440 | tf_op jit(solution)/shard_map/all_gather | solution.py:42
  159.9 1.4 stack.31
  162.2 53.6 %all_to_all.28 = f32[2,1,128,648]{3,1,0,2:T(1,128)S(1)} all-to-all(f32[2,1,128,648]{3,1,0,2:T(1,128)S(1)} %copy.73), channel_id=1, replica_groups=mesh['chan'=128,'blk'=4] {'chan'}, dimensions={2} | all-to-all | bytes 1327104 | tf_op jit(solution)/shard_map/all_to_all | solution.py:54
  220.6 2.3 copy.76
  222.9 50.7 %all_to_all.29 = f32[2,128,1,648]{3,2,0,1:T(1,128)S(1)} all-to-all(f32[2,128,1,648]{3,2,0,1:T(1,128)S(1)} %copy.76), channel_id=1, replica_groups=mesh['chan'=128,'blk'=4] {'chan'}, dimensions={1} | all-to-all | bytes 1327104 | tf_op jit(solution)/shard_map/all_to_all | solution.py:53
  273.6 1.3 fusion.42
  276.6 11.6 %all_gather.19 = bf16[1,576,576]{2,1,0:T(8,128)(2,1)S(1)} all-gather(bf16[1,144,576]{2,1,0:T(8,128)(2,1)S(1)} %convert_element_type.111), channel_id=1, replica_groups=mesh['chan'=128,'blk'=4] {'blk'}, dimensions={1}, use_global_device_ids=true | all-gather | bytes 829440 | tf_op jit(solution)/shard_map/all_gather | solution.py:42
  290.2 36.9 %all_to_all.30 = f32[1,1,128,648]{3,1,0,2:T(1,128)S(1)} all-to-all(f32[1,1,128,648]{3,1,0,2:T(1,128)S(1)} %reshape_broadcast_in_dim.4), channel_id=1, replica_groups=mesh['chan'=128,'blk'=4] {'chan'}, dimensions={2} | all-to-all | bytes 663552 | tf_op jit(solution)/shard_map/all_to_all | solution.py:54
  328.4 1.2 copy.82
  329.6 6.2 %all-to-all-start.6 = ((f32[1,128,1,648]{3,2,0,1:T(1,128)}), f32[1,128,1,648]{3,2,0,1:T(1,128)S(1)}, u32[]{:S(2)}, u32[]{:S(2)}) async-start(f32[1,128,1,648]{3,2,0,1:T(1,128)} %copy.82), calls=%async_computation.6 | async-start | bytes 786432 | tf_op jit(solution)/shard_map/all_to_all | solution.py:53
  336.5 4.4 %sort.17 = (s32[576]{0:T(1024)}, s32[576]{0:T(1024)S(1)}) sort(s32[576]{0:T(1024)S(1)} %copy-done.18, s32[576]{0:T(1024)S(1)} %iota.20), dimensions={0}, to_apply=%region_0.0 | sort | flops 5760 | bytes 9216 | tf_op jit(solution)/shard_map/jit(argsort)/sort | solution.py:76
  341.5 2.2 gather_fusion.3
  344.0 11.7 %all-gather = bf16[576,576]{1,0:T(8,128)(2,1)S(1)} all-gather(bf16[144,576]{1,0:T(8,128)(2,1)S(1)} %fusion.33), channel_id=2, replica_groups=mesh['chan'=128,'blk'=4] {'blk'}, dimensions={0}, use_global_device_ids=true | all-gather | bytes 829440 | tf_op jit(solution)/shard_map/all_gather | solution.py:42
  355.6 1.2 fusion.39
  356.8 7.2 %all-to-all-done.6 = f32[1,128,1,648]{3,2,0,1:T(1,128)S(1)} async-done(((f32[1,128,1,648]{3,2,0,1:T(1,128)}), f32[1,128,1,648]{3,2,0,1:T(1,128)S(1)}, u32[]{:S(2)}, u32[]{:S(2)}) %all-to-all-start.6) | async-done | bytes 331808 | tf_op jit(solution)/shard_map/all_to_all | solution.py:53
  365.6 2.8 gather_fusion.4
  368.4 1.3 copy.84
  (109 shorter events, 28.9 us)
Async XLA Ops:
  0.0 29.0 %copy-start = (f32[128,128]{1,0:T(8,128)S(1)}, f32[128,128]{1,0:T(8,128)}, u32[]{:S(2)}) copy-start(f32[128,128]{1,0:T(8,128)} %param.16) | copy-start | bytes 196612
  0.0 0.7 copy-start.17
  0.7 109.2 %copy-start.13 = (pred[576]{0:T(1024)(128)(4,1)}, pred[576]{0:T(1024)(128)(4,1)S(1)}, u32[]{:S(2)}) copy-start(pred[576]{0:T(1024)(128)(4,1)S(1)} %iota_compare_fusion.3) | copy-start | bytes 1732
  0.8 109.2 %copy-start.15 = (pred[144]{0:T(512)(128)(4,1)}, pred[144]{0:T(512)(128)(4,1)S(1)}, u32[]{:S(2)}) copy-start(pred[144]{0:T(512)(128)(4,1)S(1)} %add_compare_fusion) | copy-start | bytes 436
  9.6 19.5 %copy-start.21 = (s32[128]{0:T(128)S(1)}, s32[128]{0:T(128)}, u32[]{:S(2)}) copy-start(s32[128]{0:T(128)} %param.14) | copy-start | bytes 1540
  9.6 19.7 %copy-start.22 = (s32[128]{0:T(128)S(1)}, s32[128]{0:T(128)}, u32[]{:S(2)}) copy-start(s32[128]{0:T(128)} %param.15) | copy-start | bytes 1540
  9.6 64.0 %all-to-all-start = ((f32[2,1,128,648]{3,0,1,2:T(2,128)}), f32[2,1,128,648]{3,0,1,2:T(2,128)S(1)}, u32[]{:S(2)}, u32[]{:S(2)}) async-start(f32[2,1,128,648]{3,0,1,2:T(2,128)} %copy.68), calls=%async_computation | async-start | bytes 1572864 | tf_op jit(solution)/shard_map/all_to_all | solution.py:54
  76.2 6.9 %copy-start.19 = (f32[1,576]{1,0:T(1,128)S(1)}, f32[1,576]{1,0:T(1,128)}, u32[]{:S(2)}) copy-start(f32[1,576]{1,0:T(1,128)} %param.11) | copy-start | bytes 6916
  76.2 51.1 %all-to-all-start.1 = ((f32[2,128,1,648]{3,0,2,1:T(2,128)}), f32[2,128,1,648]{3,0,2,1:T(2,128)}, u32[]{:S(2)}, u32[]{:S(2)}) async-start(f32[2,128,1,648]{3,0,2,1:T(2,128)} %copy.70), calls=%async_computation.1 | async-start | bytes 1572864 | tf_op jit(solution)/shard_map/all_to_all | solution.py:53
  83.1 0.7 copy-start.20
  83.8 1.0 copy-start.1
  83.8 1.1 copy-start.2
  84.9 46.3 %copy-start.3 = (f32[1,128,1,648]{3,1,2,0:T(8,128)}, f32[1,128,1,648]{3,1,2,0:T(8,128)S(1)}, u32[]{:S(2)}) copy-start(f32[1,128,1,648]{3,1,2,0:T(8,128)S(1)} %mul.105) | copy-start | bytes 995332
  134.2 23.7 %copy-start.5 = (bf16[144,576]{1,0:T(8,128)(2,1)}, bf16[144,576]{1,0:T(8,128)(2,1)S(1)}, u32[]{:S(2)}) copy-start(bf16[144,576]{1,0:T(8,128)(2,1)S(1)} %convert_element_type.102) | copy-start | bytes 497668
  135.2 4.3 %copy-start.12 = (bf16[1,144,576]{2,1,0:T(8,128)(2,1)S(1)}, bf16[1,144,576]{2,1,0:T(8,128)(2,1)}, u32[]{:S(2)}) copy-start(bf16[1,144,576]{2,1,0:T(8,128)(2,1)} %convert_element_type.104) | copy-start | bytes 497668
  135.2 23.0 %all-to-all-start.2 = ((bf16[4,1,144,576]{3,2,1,0:T(8,128)(2,1)}), bf16[4,1,144,576]{3,2,1,0:T(8,128)(2,1)S(1)}, u32[]{:S(2)}, u32[]{:S(2)}) async-start(bf16[4,1,144,576]{3,2,1,0:T(8,128)(2,1)} %broadcast_in_dim.7), calls=%async_computation.2 | async-start | bytes 1474560 | tf_op jit(solution)/shard_map/all_to_all | solution.py:17
  157.9 0.9 copy-start.10
  159.9 1.4 copy-start.7
  218.0 1.0 copy-start.9
  273.6 1.3 copy-start.4
  276.6 11.6 %copy-start.6 = (bf16[144,576]{1,0:T(8,128)(2,1)S(1)}, bf16[144,576]{1,0:T(8,128)(2,1)}, u32[]{:S(2)}) copy-start(bf16[144,576]{1,0:T(8,128)(2,1)} %copy-done.5) | copy-start | bytes 497668
  288.2 0.9 copy-start.11
  329.6 34.4 %all-to-all-start.6 = ((f32[1,128,1,648]{3,2,0,1:T(1,128)}), f32[1,128,1,648]{3,2,0,1:T(1,128)S(1)}, u32[]{:S(2)}, u32[]{:S(2)}) async-start(f32[1,128,1,648]{3,2,0,1:T(1,128)} %copy.82), calls=%async_computation.6 | async-start | bytes 786432 | tf_op jit(solution)/shard_map/all_to_all | solution.py:53
  335.8 0.7 copy-start.18
  343.9 11.7 %copy-start.14 = (pred[576]{0:T(1024)(128)(4,1)S(1)}, pred[576]{0:T(1024)(128)(4,1)}, u32[]{:S(2)}) copy-start(pred[576]{0:T(1024)(128)(4,1)} %copy-done.13) | copy-start | bytes 1732
  343.9 11.7 %copy-start.16 = (pred[144]{0:T(512)(128)(4,1)S(1)}, pred[144]{0:T(512)(128)(4,1)}, u32[]{:S(2)}) copy-start(pred[144]{0:T(512)(128)(4,1)} %copy-done.15) | copy-start | bytes 436
  368.4 1.3 copy-start.8
where the time goes:
time: 372 us; the launch traced here: 371 us
  blocking collectives  207 us (56%)
  waiting for transfers between devices  64.5 us (17%)
  local copies, waits for them, and re-layouts  44.6 us (12%)
  starting transfers between devices  36.8 us (10%)
  matrix products  8.37 us (2%)
  other arithmetic  7.91 us (2%)
    all_to_all x2, blocking collectives, through_mixing(): lax.all_to_all(shaped, 'chan', split_axis=2, concat_axis=1, tiled=True)  90.5 us
    all_gather x4, blocking collectives, commutator(): lax.all_gather(right_rows.astype(jnp.bfloat16), 'blk', axis=1, tiled=True)  53.7 us
    all_to_all x1, blocking collectives, through_mixing(): lax.all_to_all(apply_fn(lax.all_to_all(shaped, 'chan', split_axis=2, conc...  50.7 us
    all_to_all x1, waiting for transfers between devices, through_mixing(): lax.all_to_all(shaped, 'chan', split_axis=2, concat_axis=1, tiled=True)  44 us
    all_to_all x2, waiting for transfers between devices, through_mixing(): lax.all_to_all(apply_fn(lax.all_to_all(shaped, 'chan', split_axis=2, conc...  20.4 us
    all_to_all x1, starting transfers between devices, through_mixing(): lax.all_to_all(shaped, 'chan', split_axis=2, concat_axis=1, tiled=True)  19.4 us
    all_to_all x2, starting transfers between devices, through_mixing(): lax.all_to_all(apply_fn(lax.all_to_all(shaped, 'chan', split_axis=2, conc...  13 us
    all_gather x1, blocking collectives, on_device(): lax.all_gather(generator.astype(jnp.bfloat16), 'blk', axis=1, tiled=True)  12.4 us
  transfers between devices with their start and end apart: 4, of which 3 were waited for; matrix products, arithmetic and copies ran while one was open for 4% of the time, Pallas kernels for 0%

commit v1 on v0

--- a/solution.py
+++ b/solution.py
@@ -98,7 +98,12 @@
     )
     gen_cross = crossed[0]
     ham_cross = crossed[1]
-    gen_full = lax.all_gather(generator.astype(jnp.bfloat16), "blk", axis=1, tiled=True)
+    gen_full = jnp.concatenate(
+        lax.all_to_all(
+            jnp.stack([generator.astype(jnp.bfloat16)] * lax.axis_size("blk")), "blk", 0, 0
+        ),
+        axis=1,
+    )
     first_pp = commutator(generator, gen_full, start_ham, pair_occ)
     cross_full = gather_directly(gen_cross.astype(jnp.bfloat16), "blk", 1)
     first_cc = commutator(gen_cross, cross_full, ham_cross, cross_occ)

time: 372 us -> 386 us (1.038)
  waiting for transfers between devices: 64.5 us -> 85.6 us
  blocking collectives: 207 us -> 195 us
  starting transfers between devices: 36.8 us -> 40.9 us
    all_to_all x2, waiting for transfers between devices: 20.4 us -> 33.4 us  [through_mixing(): lax.all_to_all(apply_fn(lax.all_to_all(shaped, 'chan', split_axis=2, conc...]
    all_gather x1 -> x0, blocking collectives: 12.4 us -> none  [on_device(): lax.all_gather(generator.astype(jnp.bfloat16), 'blk', axis=1, tiled=True)]
    all_to_all x0 -> x1, waiting for transfers between devices: none -> 8.45 us  [on_device(): lax.all_to_all(jnp.stack([generator.astype(jnp.bfloat16)] * lax.axis_size...]
    all_to_all x0 -> x1, starting transfers between devices: none -> 4.31 us  [on_device(): lax.all_to_all(jnp.stack([generator.astype(jnp.bfloat16)] * lax.axis_size...]
  transfers between devices with their start and end apart: 4 -> 5, of which waited for: 3 -> 4; matrix products, arithmetic and copies ran while one was open for 4% -> 5% of each run, Pallas kernels for 0% -> 0%
where the time goes in v1:
time: 386 us; the launch traced here: 385 us
  blocking collectives  195 us (51%)
  waiting for transfers between devices  85.6 us (22%)
  local copies, waits for them, and re-layouts  45.4 us (12%)
  starting transfers between devices  40.9 us (11%)
  other arithmetic  8.61 us (2%)
  matrix products  8.37 us (2%)
    all_to_all x2, blocking collectives, through_mixing(): lax.all_to_all(shaped, 'chan', split_axis=2, concat_axis=1, tiled=True)  89.8 us
    all_gather x4, blocking collectives, commutator(): lax.all_gather(right_rows.astype(jnp.bfloat16), 'blk', axis=1, tiled=True)  54 us
    all_to_all x1, blocking collectives, through_mixing(): lax.all_to_all(apply_fn(lax.all_to_all(shaped, 'chan', split_axis=2, conc...  50.7 us
    all_to_all x1, waiting for transfers between devices, through_mixing(): lax.all_to_all(shaped, 'chan', split_axis=2, concat_axis=1, tiled=True)  43.8 us
    all_to_all x2, waiting for transfers between devices, through_mixing(): lax.all_to_all(apply_fn(lax.all_to_all(shaped, 'chan', split_axis=2, conc...  33.4 us
    all_to_all x1, starting transfers between devices, through_mixing(): lax.all_to_all(shaped, 'chan', split_axis=2, concat_axis=1, tiled=True)  19.4 us
    all_to_all x2, starting transfers between devices, through_mixing(): lax.all_to_all(apply_fn(lax.all_to_all(shaped, 'chan', split_axis=2, conc...  13.5 us
    all_to_all x1, waiting for transfers between devices, on_device(): lax.all_to_all(jnp.stack([generator.astype(jnp.bfloat16)] * lax.axis_size...  8.45 us
  transfers between devices with their start and end apart: 5, of which 4 were waited for; matrix products, arithmetic and copies ran while one was open for 5% of the time, Pallas kernels for 0%

profile of v1, /device:TPU:33, one launch (start us, length us, event | category | flops | bytes accessed | tf_op | source)
XLA Modules:
  0.0 384.7 jit_solution(16500995667496572938)
XLA Ops:
  0.8 1.2 fusion.19
  2.2 2.2 gather_fusion.1
  5.2 2.2 gather_fusion.2
  8.1 1.5 copy.68
  9.6 19.4 %all-to-all-start.1 = ((f32[2,1,128,648]{3,0,1,2:T(2,128)}), f32[2,1,128,648]{3,0,1,2:T(2,128)S(1)}, u32[]{:S(2)}, u32[]{:S(2)}) async-start(f32[2,1,128,648]{3,0,1,2:T(2,128)} %copy.68), calls=%async_computation.1 | async-start | bytes 1572864 | tf_op jit(solution)/shard_map/all_to_all | solution.py:54
  29.8 43.8 %all-to-all-done.1 = f32[2,1,128,648]{3,0,1,2:T(2,128)S(1)} async-done(((f32[2,1,128,648]{3,0,1,2:T(2,128)}), f32[2,1,128,648]{3,0,1,2:T(2,128)S(1)}, u32[]{:S(2)}, u32[]{:S(2)}) %all-to-all-start.1) | async-done | bytes 663584 | tf_op jit(solution)/shard_map/all_to_all | solution.py:54
  74.6 4.3 %all-to-all-start = ((bf16[4,1,144,576]{3,2,1,0:T(8,128)(2,1)}), bf16[4,1,144,576]{3,2,1,0:T(8,128)(2,1)S(1)}, u32[]{:S(2)}, u32[]{:S(2)}) async-start(bf16[4,1,144,576]{3,2,1,0:T(8,128)(2,1)} %stack.34), calls=%async_computation | async-start | bytes 1474560 | tf_op jit(solution)/shard_map/all_to_all | solution.py:102
  80.7 1.3 copy.70
  82.0 8.5 %all-to-all-done = bf16[4,1,144,576]{3,2,1,0:T(8,128)(2,1)S(1)} async-done(((bf16[4,1,144,576]{3,2,1,0:T(8,128)(2,1)}), bf16[4,1,144,576]{3,2,1,0:T(8,128)(2,1)S(1)}, u32[]{:S(2)}, u32[]{:S(2)}) %all-to-all-start) | async-done | bytes 663584 | tf_op jit(solution)/shard_map/all_to_all | solution.py:102
  90.5 7.3 %all-to-all-start.2 = ((f32[2,128,1,648]{3,0,2,1:T(2,128)}), f32[2,128,1,648]{3,0,2,1:T(2,128)}, u32[]{:S(2)}, u32[]{:S(2)}) async-start(f32[2,128,1,648]{3,0,2,1:T(2,128)} %copy.70), calls=%async_computation.2 | async-start | bytes 1572864 | tf_op jit(solution)/shard_map/all_to_all | solution.py:53
  99.5 11.9 %all_gather.12 = bf16[1,576,576]{2,1,0:T(8,128)(2,1)S(1)} all-gather(bf16[1,144,576]{2,1,0:T(8,128)(2,1)S(1)} %copy-done.10), channel_id=1, replica_groups=mesh['chan'=128,'blk'=4] {'blk'}, dimensions={1}, use_global_device_ids=true | all-gather | bytes 829440 | tf_op jit(solution)/shard_map/all_gather | solution.py:42
  112.4 2.2 gather_fusion
  115.9 26.2 %all-to-all-done.2 = f32[2,128,1,648]{3,0,2,1:T(2,128)} async-done(((f32[2,128,1,648]{3,0,2,1:T(2,128)}), f32[2,128,1,648]{3,0,2,1:T(2,128)}, u32[]{:S(2)}, u32[]{:S(2)}) %all-to-all-start.2) | async-done | bytes 663584 | tf_op jit(solution)/shard_map/all_to_all | solution.py:53
  142.1 2.1 fusion.43
  146.1 1.4 convert_element_type.103
  149.9 3.6 all-to-all-start.3
  153.6 18.9 %all_gather.13 = bf16[1,576,576]{2,1,0:T(8,128)(2,1)S(1)} all-gather(bf16[1,144,576]{2,1,0:T(8,128)(2,1)S(1)} %copy-done.13), channel_id=1, replica_groups=mesh['chan'=128,'blk'=4] {'blk'}, dimensions={1}, use_global_device_ids=true | all-gather | bytes 829440 | tf_op jit(solution)/shard_map/all_gather | solution.py:42
  174.5 1.4 stack.39
  176.8 52.9 %all_to_all.64 = f32[2,1,128,648]{3,1,0,2:T(1,128)S(1)} all-to-all(f32[2,1,128,648]{3,1,0,2:T(1,128)S(1)} %copy.73), channel_id=1, replica_groups=mesh['chan'=128,'blk'=4] {'chan'}, dimensions={2} | all-to-all | bytes 1327104 | tf_op jit(solution)/shard_map/all_to_all | solution.py:54
  234.4 2.3 copy.76
  236.7 50.7 %all_to_all.65 = f32[2,128,1,648]{3,2,0,1:T(1,128)S(1)} all-to-all(f32[2,128,1,648]{3,2,0,1:T(1,128)S(1)} %copy.76), channel_id=1, replica_groups=mesh['chan'=128,'blk'=4] {'chan'}, dimensions={1} | all-to-all | bytes 1327104 | tf_op jit(solution)/shard_map/all_to_all | solution.py:53
  287.4 1.3 fusion.41
  290.4 11.6 %all_gather.15 = bf16[1,576,576]{2,1,0:T(8,128)(2,1)S(1)} all-gather(bf16[1,144,576]{2,1,0:T(8,128)(2,1)S(1)} %convert_element_type.114), channel_id=1, replica_groups=mesh['chan'=128,'blk'=4] {'blk'}, dimensions={1}, use_global_device_ids=true | all-gather | bytes 829440 | tf_op jit(solution)/shard_map/all_gather | solution.py:42
  304.0 36.9 %all_to_all.66 = f32[1,1,128,648]{3,1,0,2:T(1,128)S(1)} all-to-all(f32[1,1,128,648]{3,1,0,2:T(1,128)S(1)} %reshape_broadcast_in_dim.4), channel_id=1, replica_groups=mesh['chan'=128,'blk'=4] {'chan'}, dimensions={2} | all-to-all | bytes 663552 | tf_op jit(solution)/shard_map/all_to_all | solution.py:54
  342.2 1.2 copy.82
  343.5 6.2 %all-to-all-start.7 = ((f32[1,128,1,648]{3,2,0,1:T(1,128)}), f32[1,128,1,648]{3,2,0,1:T(1,128)S(1)}, u32[]{:S(2)}, u32[]{:S(2)}) async-start(f32[1,128,1,648]{3,2,0,1:T(1,128)} %copy.82), calls=%async_computation.7 | async-start | bytes 786432 | tf_op jit(solution)/shard_map/all_to_all | solution.py:53
  350.4 4.4 %sort.17 = (s32[576]{0:T(1024)}, s32[576]{0:T(1024)S(1)}) sort(s32[576]{0:T(1024)S(1)} %copy-done.19, s32[576]{0:T(1024)S(1)} %iota.20), dimensions={0}, to_apply=%region_0.0 | sort | flops 5760 | bytes 9216 | tf_op jit(solution)/shard_map/jit(argsort)/sort | solution.py:76
  355.4 2.2 gather_fusion.3
  357.8 11.7 %all-gather = bf16[576,576]{1,0:T(8,128)(2,1)S(1)} all-gather(bf16[144,576]{1,0:T(8,128)(2,1)S(1)} %fusion.32), channel_id=2, replica_groups=mesh['chan'=128,'blk'=4] {'blk'}, dimensions={0}, use_global_device_ids=true | all-gather | bytes 829440 | tf_op jit(solution)/shard_map/all_gather | solution.py:42
  370.6 7.2 %all-to-all-done.7 = f32[1,128,1,648]{3,2,0,1:T(1,128)S(1)} async-done(((f32[1,128,1,648]{3,2,0,1:T(1,128)}), f32[1,128,1,648]{3,2,0,1:T(1,128)S(1)}, u32[]{:S(2)}, u32[]{:S(2)}) %all-to-all-start.7) | async-done | bytes 331808 | tf_op jit(solution)/shard_map/all_to_all | solution.py:53
  379.4 2.8 gather_fusion.4
  382.2 1.3 copy.84
  (113 shorter events, 31.5 us)
Async XLA Ops:
  0.0 78.9 %copy-start = (f32[128,128]{1,0:T(8,128)S(1)}, f32[128,128]{1,0:T(8,128)}, u32[]{:S(2)}) copy-start(f32[128,128]{1,0:T(8,128)} %param.16) | copy-start | bytes 196612
  0.0 0.7 copy-start.18
  0.7 111.0 %copy-start.14 = (pred[576]{0:T(1024)(128)(4,1)}, pred[576]{0:T(1024)(128)(4,1)S(1)}, u32[]{:S(2)}) copy-start(pred[576]{0:T(1024)(128)(4,1)S(1)} %iota_compare_fusion.3) | copy-start | bytes 1732
  0.8 111.0 %copy-start.16 = (pred[144]{0:T(512)(128)(4,1)}, pred[144]{0:T(512)(128)(4,1)S(1)}, u32[]{:S(2)}) copy-start(pred[144]{0:T(512)(128)(4,1)S(1)} %add_compare_fusion) | copy-start | bytes 436
  9.5 19.5 %copy-start.1 = (f32[1,144,576]{2,1,0:T(8,128)S(1)}, f32[1,144,576]{2,1,0:T(8,128)}, u32[]{:S(2)}) copy-start(f32[1,144,576]{2,1,0:T(8,128)} %param.10) | copy-start | bytes 995332
  9.6 19.5 %copy-start.2 = (f32[1,144,576]{2,1,0:T(8,128)S(1)}, f32[1,144,576]{2,1,0:T(8,128)}, u32[]{:S(2)}) copy-start(f32[1,144,576]{2,1,0:T(8,128)} %param.9) | copy-start | bytes 995332
  9.6 64.0 %all-to-all-start.1 = ((f32[2,1,128,648]{3,0,1,2:T(2,128)}), f32[2,1,128,648]{3,0,1,2:T(2,128)S(1)}, u32[]{:S(2)}, u32[]{:S(2)}) async-start(f32[2,1,128,648]{3,0,1,2:T(2,128)} %copy.68), calls=%async_computation.1 | async-start | bytes 1572864 | tf_op jit(solution)/shard_map/all_to_all | solution.py:54
  74.6 4.3 %copy-start.22 = (s32[128]{0:T(128)S(1)}, s32[128]{0:T(128)}, u32[]{:S(2)}) copy-start(s32[128]{0:T(128)} %param.14) | copy-start | bytes 1540
  74.6 4.6 %copy-start.23 = (s32[128]{0:T(128)S(1)}, s32[128]{0:T(128)}, u32[]{:S(2)}) copy-start(s32[128]{0:T(128)} %param.15) | copy-start | bytes 1540
  74.6 15.9 %all-to-all-start = ((bf16[4,1,144,576]{3,2,1,0:T(8,128)(2,1)}), bf16[4,1,144,576]{3,2,1,0:T(8,128)(2,1)S(1)}, u32[]{:S(2)}, u32[]{:S(2)}) async-start(bf16[4,1,144,576]{3,2,1,0:T(8,128)(2,1)} %stack.34), calls=%async_computation | async-start | bytes 1474560 | tf_op jit(solution)/shard_map/all_to_all | solution.py:102
  82.0 15.7 %copy-start.20 = (f32[1,576]{1,0:T(1,128)S(1)}, f32[1,576]{1,0:T(1,128)}, u32[]{:S(2)}) copy-start(f32[1,576]{1,0:T(1,128)} %param.11) | copy-start | bytes 6916
  90.5 51.6 %all-to-all-start.2 = ((f32[2,128,1,648]{3,0,2,1:T(2,128)}), f32[2,128,1,648]{3,0,2,1:T(2,128)}, u32[]{:S(2)}, u32[]{:S(2)}) async-start(f32[2,128,1,648]{3,0,2,1:T(2,128)} %copy.70), calls=%async_computation.2 | async-start | bytes 1572864 | tf_op jit(solution)/shard_map/all_to_all | solution.py:53
  97.8 0.7 copy-start.21
  98.5 0.9 copy-start.10
  98.9 47.1 %copy-start.3 = (f32[1,128,1,648]{3,1,2,0:T(8,128)}, f32[1,128,1,648]{3,1,2,0:T(8,128)S(1)}, u32[]{:S(2)}) copy-start(f32[1,128,1,648]{3,1,2,0:T(8,128)S(1)} %mul.105) | copy-start | bytes 995332
  149.0 23.5 %copy-start.5 = (bf16[144,576]{1,0:T(8,128)(2,1)}, bf16[144,576]{1,0:T(8,128)(2,1)S(1)}, u32[]{:S(2)}) copy-start(bf16[144,576]{1,0:T(8,128)(2,1)S(1)} %convert_element_type.105) | copy-start | bytes 497668
  149.9 3.6 copy-start.13
  149.9 22.9 %all-to-all-start.3 = ((bf16[4,1,144,576]{3,2,1,0:T(8,128)(2,1)}), bf16[4,1,144,576]{3,2,1,0:T(8,128)(2,1)S(1)}, u32[]{:S(2)}, u32[]{:S(2)}) async-start(bf16[4,1,144,576]{3,2,1,0:T(8,128)(2,1)} %broadcast_in_dim.7), calls=%async_computation.3 | async-start | bytes 1474560 | tf_op jit(solution)/shard_map/all_to_all | solution.py:17
  172.5 0.9 copy-start.11
  174.5 1.4 copy-start.7
  231.8 1.0 copy-start.9
  287.4 1.3 copy-start.4
  290.4 11.6 %copy-start.6 = (bf16[144,576]{1,0:T(8,128)(2,1)S(1)}, bf16[144,576]{1,0:T(8,128)(2,1)}, u32[]{:S(2)}) copy-start(bf16[144,576]{1,0:T(8,128)(2,1)} %copy-done.5) | copy-start | bytes 497668
  302.0 0.9 copy-start.12
  343.5 34.4 %all-to-all-start.7 = ((f32[1,128,1,648]{3,2,0,1:T(1,128)}), f32[1,128,1,648]{3,2,0,1:T(1,128)S(1)}, u32[]{:S(2)}, u32[]{:S(2)}) async-start(f32[1,128,1,648]{3,2,0,1:T(1,128)} %copy.82), calls=%async_computation.7 | async-start | bytes 786432 | tf_op jit(solution)/shard_map/all_to_all | solution.py:53
  349.7 0.7 copy-start.19
  357.8 11.7 %copy-start.15 = (pred[576]{0:T(1024)(128)(4,1)S(1)}, pred[576]{0:T(1024)(128)(4,1)}, u32[]{:S(2)}) copy-start(pred[576]{0:T(1024)(128)(4,1)} %copy-done.14) | copy-start | bytes 1732
  357.8 11.7 %copy-start.17 = (pred[144]{0:T(512)(128)(4,1)S(1)}, pred[144]{0:T(512)(128)(4,1)}, u32[]{:S(2)}) copy-start(pred[144]{0:T(512)(128)(4,1)} %copy-done.16) | copy-start | bytes 436
  382.2 1.3 copy-start.8
